TPU v7x, 32 devices: a whole 2x2x4 slice. The times are simulated.
32 devices in a mesh: img: 4 (over y, x), cap: 8 (over z, core).
Axes of the slice: x: 2, y: 2, z: 4, core: 2. Of those that a mesh axis runs over, the one named last changes fastest.
Arguments:
- images: float32 [8192, 768], P('img'), may hold values from -100 to 100
- captions: float32 [8192, 768], P('cap', 'img'), may hold values from -8 to 8
- bank: float32 [8192, 768], P('img'), may hold values from -100 to 100
Outputs:
- expected: float32 [8192, 768], P('img')
All inputs are finite; a program needn't handle non-finite values.
Results may differ from a plain program's by a relative error of at most 0.0003.
Values sent between devices are 32-bit elements; how exact they have to be, the bound alone decides.
A program may use at most 448 MiB of HBM per device.

v0:
```python
import jax
import jax.numpy as jnp
from jax import lax
from jax.sharding import PartitionSpec as P

exponent_divisor = 0.03


def similar(query_factor, target_factor):
    return exponent_divisor * lax.dot_general(
        query_factor,
        target_factor,
        (((1,), (1,)), ((), ())),
        precision=lax.Precision.HIGHEST,
        preferred_element_type=jnp.float32,
    )


def rescaled_affinity(weights, features):
    return jnp.dot(
        weights, features, precision=lax.Precision.HIGHEST, preferred_element_type=jnp.float32
    )


def local(images, captions, bank):
    features = lax.all_gather(captions, "img", axis=1, tiled=True)
    querybank_similarity = similar(bank, features)
    local_peak = jnp.max(querybank_similarity, axis=0)
    peak = lax.pmax(local_peak, "img")
    total = lax.psum(jnp.sum(jnp.exp(querybank_similarity - peak[None, :]), axis=0), "img")
    col_log = peak + jnp.log(total)
    logits = similar(images, features) - col_log[None, :]
    row_peak = jnp.max(logits, axis=1)
    top = lax.pmax(row_peak, "cap")
    weights = jnp.exp(logits - top[:, None])
    summed, row_total = lax.psum(
        (rescaled_affinity(weights, features), jnp.sum(weights, axis=1)), "cap"
    )
    result = summed / row_total[:, None]
    return result


def solution(mesh):
    return jax.shard_map(
        local,
        mesh=mesh,
        in_specs=(P("img", None), P("cap", "img"), P("img", None)),
        out_specs=P("img", None),
        check_vma=False,
    )
```

profile of v0, /device:TPU:0, one launch (start us, length us, event | category | flops | bytes accessed | tf_op | source)
XLA Modules:
  0.0 349.1 jit_solution(13348303251154568632)
XLA Ops:
  6.5 0.0 all-gather.2.cloned.1.call-start
  6.5 0.7 all-gather.2.cloned.1.call-update
  7.3 0.0 all-reduce.2.cloned.1.call-start
  7.3 48.6 %all-gather.2.cloned.1.call-done = f32[1024,768]{0,1:T(8,128)} async-done(((f32[1024,192]{0,1:T(8,128)}), f32[1024,768]{0,1:T(8,128)}) %all-gather.2.cloned.1.call-update) | async-done | bytes 3145744 | tf_op jit(solution)/shard_map/all_gather | solution.py:26
  55.9 25.2 %multiply_reduce_fusion = (f32[1024]{0:T(1024)S(1)}, f32[2048,1024]{0,1:T(8,128)}) fusion(f32[2048,768]{1,0:T(8,128)} %param.5, f32[1024,768]{0,1:T(8,128)} %all-gather.2.cloned.1.call-done), kind=kOutput, calls=%fused_computation.3 | convolution fusion | flops 19331547136 | bytes 17829888 | tf_op jit(solution)/shard_map/dot_general | solution.py:10
  81.1 0.0 copy-start
  81.1 9.4 %pmax.14 = f32[1024]{0:T(1024)S(1)} all-reduce(f32[1024]{0:T(1024)S(1)} %get-tuple-element.5), channel_id=1, replica_groups=mesh['img'=4,'cap'=8] {'img'}, use_global_device_ids=true, to_apply=%region_1.0 | all-reduce | flops 1024 | bytes 8192 | tf_op jit(solution)/shard_map/pmax | solution.py:29
  90.5 4.4 %exponential_reduce_fusion = f32[1024]{0:T(1024)S(1)} fusion(f32[2048,1024]{0,1:T(8,128)} %get-tuple-element.6, f32[1024]{0:T(1024)S(1)} %pmax.14), kind=kLoop, calls=%fused_computation.1 | loop fusion | flops 6290432 | bytes 8396800 | tf_op jit(solution)/shard_map/reduce_sum | solution.py:30
  94.9 8.9 %psum.21 = f32[1024]{0:T(1024)S(1)} all-reduce(f32[1024]{0:T(1024)S(1)} %exponential_reduce_fusion), channel_id=1, replica_groups=mesh['img'=4,'cap'=8] {'img'}, use_global_device_ids=true, to_apply=%region_3.0 | all-reduce | flops 1024 | bytes 8192 | tf_op jit(solution)/shard_map/psum | solution.py:30
  103.8 0.0 copy-done
  103.8 25.2 %fusion = (f32[2048]{0:T(1024)S(1)}, f32[2048,1024]{0,1:T(8,128)}) fusion(f32[1024]{0:T(1024)S(1)} %log_add_fusion, f32[2048,768]{1,0:T(8,128)} %param.3, f32[1024,768]{0,1:T(8,128)S(1)} %copy-done), kind=kOutput, calls=%fused_computation.4 | convolution fusion | flops 19333642240 | bytes 17838080 | tf_op jit(solution)/shard_map/dot_general | solution.py:10
  129.0 13.9 %pmax.15 = f32[2048]{0:T(1024)S(1)} all-reduce(f32[2048]{0:T(1024)S(1)} %get-tuple-element.7), channel_id=1, replica_groups=mesh['img'=4,'cap'=8] {'cap'}, use_global_device_ids=true, to_apply=%region_5.0 | all-reduce | flops 2048 | bytes 16384 | tf_op jit(solution)/shard_map/pmax | solution.py:34
  142.9 59.2 %fusion.2 = f32[2048,768]{1,0:T(8,128)} fusion(f32[1024,768]{0,1:T(8,128)S(1)} %copy-done, f32[2048,1024]{0,1:T(8,128)} %get-tuple-element.8, f32[2048]{0:T(1024)S(1)} %pmax.15, f32[1024]{0:T(1024)S(1)} %log_add_fusion), kind=kOutput, calls=%fused_computation.6 | convolution fusion | flops 19333644288 | bytes 17838080 | tf_op jit(solution)/shard_map/dot_general | solution.py:20
  202.1 0.0 all-reduce.2.cloned.1.call-update
  202.1 5.1 %fusion.1 = f32[2048]{0:T(1024)S(1)} fusion(f32[2048,1024]{0,1:T(8,128)} %get-tuple-element.8, f32[2048]{0:T(1024)S(1)} %pmax.15, f32[1024]{0:T(1024)S(1)} %log_add_fusion), kind=kLoop, calls=%fused_computation.5 | loop fusion | flops 8386560 | bytes 8409088 | tf_op jit(solution)/shard_map/reduce_sum | solution.py:37
  207.2 14.9 %psum.23 = f32[2048]{0:T(1024)S(1)} all-reduce(f32[2048]{0:T(1024)S(1)} %fusion.1), channel_id=1, replica_groups=mesh['img'=4,'cap'=8] {'cap'}, use_global_device_ids=true, to_apply=%region_8.0 | all-reduce | flops 2048 | bytes 16384 | tf_op jit(solution)/shard_map/psum | solution.py:36
  222.1 114.1 %all-reduce.2.cloned.1.call-done = f32[2048,768]{1,0:T(8,128)} async-done(((f32[2048,768]{1,0:T(8,128)}), f32[2048,768]{1,0:T(8,128)}) %all-reduce.2.cloned.1.call-update) | async-done | bytes 6291472 | tf_op jit(solution)/shard_map/psum | solution.py:36
  336.1 6.0 %broadcast_divide_fusion = f32[2048,768]{1,0:T(8,128)} fusion(f32[2048,768]{1,0:T(8,128)} %all-reduce.2.cloned.1.call-done, f32[2048]{0:T(1024)S(1)} %psum.23), kind=kLoop, calls=%fused_computation.10 | loop fusion | flops 1572864 | bytes 12591104 | tf_op jit(solution)/shard_map/div | solution.py:39
  (1 shorter events, 0.0 us)
Async XLA Ops:
  6.5 49.4 %all-gather.2.cloned.1.call-start = ((), (), s32[]{:S(2)}) async-start(), calls=%async_computation | async-start | bytes 3932160 | tf_op jit(solution)/shard_map/all_gather | solution.py:26
  7.3 328.9 %all-reduce.2.cloned.1.call-start = ((), (), s32[]{:S(2)}) async-start(), calls=%async_computation.1 | async-start | bytes 12582912 | tf_op jit(solution)/shard_map/psum | solution.py:36
  81.1 22.7 %copy-start = (f32[1024,768]{0,1:T(8,128)S(1)}, f32[1024,768]{0,1:T(8,128)}, u32[]{:S(2)}) copy-start(f32[1024,768]{0,1:T(8,128)} %all-gather.2.cloned.1.call-done) | copy-start | bytes 9437188
Sparse Core Ops, SparseCore 0:
  9.2 46.6 all-gather.1
  202.2 133.8 all-reduce.1
where the time goes:
time: 350 us; the launch traced here: 349 us
  waiting for transfers between devices  163 us (47%)
  matrix products  110 us (31%)
  blocking collectives  47 us (13%)
  other arithmetic  15.4 us (4%)
  between operations  13.6 us (4%)
    psum x1, waiting for transfers between devices, local(): lax.psum((rescaled_affinity(weights, features), jnp.sum(weights, axis=1))...  114 us
    dot_general x1, matrix products, rescaled_affinity(): jnp.dot(weights, features, precision=lax.Precision.HIGHEST, preferred_ele...  59.2 us
    dot_general x2, matrix products, similar(): lax.dot_general(query_factor, target_factor, (((1,), (1,)), ((), ())), pr...  50.4 us
    all_gather x1, waiting for transfers between devices, local(): features = lax.all_gather(captions, 'img', axis=1, tiled=True)  48.6 us
    psum x1, blocking collectives, local(): lax.psum((rescaled_affinity(weights, features), jnp.sum(weights, axis=1))...  14.9 us
    pmax x1, blocking collectives, local(): top = lax.pmax(row_peak, 'cap')  13.9 us
    pmax x1, blocking collectives, local(): peak = lax.pmax(local_peak, 'img')  9.4 us
    psum x1, blocking collectives, local(): lax.psum(jnp.sum(jnp.exp(querybank_similarity - peak[None, :]), axis=0),...  8.88 us
  transfers between devices with their start and end apart: 2, of which 2 were waited for; matrix products, arithmetic and copies ran while one was open for 1% of the time, Pallas kernels for 0%

commit v1 on v0

v1 whole, which is shorter than its diff:
```python
import functools

import jax
import jax.numpy as jnp
from jax import lax
from jax.experimental import pallas as pl
from jax.experimental.pallas import tpu as pltpu
from jax.sharding import PartitionSpec as P

SCALE = 0.03
CW = 256
RB = 512
RC = 32
LAG = 2
F32 = jnp.float32
BF16 = jnp.bfloat16


def split(x):
    hi = x.astype(BF16)
    return hi, (x - hi.astype(F32)).astype(BF16)


def loop(count, body):
    def step(i, carry):
        body(i)
        return carry

    lax.fori_loop(0, count, step, 0)


def kernel(
    n, chips, images, bank, cap, out,
    rows_f, rows_h, rows_l, cap_f, cap_h, cap_l, scores, acc, red, fin,
    stats, collog, ml, factor,
    load_sem, ring_send, ring_recv, sib_send, sib_recv, st_send, st_recv, ml_send, ml_recv,
    red_send, red_recv, bc_send, bc_recv, os_send, os_recv, loc_sem,
):
    fs, cl = cap.shape
    d = n * fs
    half = images.shape[0] // 2
    k_n = cl // CW
    side = half // 2
    t_n = side // RC
    eye = (
        lax.broadcasted_iota(jnp.int32, (128, 128), 0)
        == lax.broadcasted_iota(jnp.int32, (128, 128), 1)
    )

    i = lax.axis_index("img")
    q = lax.axis_index("cap")
    core = q % 2
    z = q // 2
    sibling = q + 1 - 2 * core
    group = i * 2 + core

    def snake(p):
        return p + (p // (n // 2)) * (3 * n // 2 - 1 - 2 * p)

    pos = snake(i)
    right = snake((pos + 1) % n)
    left = snake((pos + n - 1) % n)

    def remote(src, dst, send, recv, device):
        return pltpu.make_async_remote_copy(
            src_ref=src, dst_ref=dst, send_sem=send, recv_sem=recv,
            device_id=device, device_id_type=pl.DeviceIdType.MESH,
        )

    def group_member(offset):
        g = (group + offset) % (2 * n)
        return (g // 2, z * 2 + g % 2)

    def chip_member(offset):
        return (i, ((z + offset) % chips) * 2 + core)

    loads = [
        pltpu.make_async_copy(
            ref.at[pl.ds(pl.multiple_of(core * half, half), half), :], rows_f.at[a], load_sem.at[a]
        )
        for a, ref in enumerate((bank, images))
    ]
    for copy in loads:
        copy.start()

    barrier = pltpu.get_barrier_semaphore()
    for offset in range(1, 2 * n):
        pl.semaphore_signal(barrier, inc=1, device_id=group_member(offset), device_id_type=pl.DeviceIdType.MESH)
    for offset in range(1, chips):
        pl.semaphore_signal(barrier, inc=1, device_id=chip_member(offset), device_id_type=pl.DeviceIdType.MESH)

    own_rows = pl.ds(pl.multiple_of(i * fs, fs), fs)
    for k in range(k_n):
        cap_f[core, k, own_rows, :] = cap[:, k * CW:(k + 1) * CW]
    pl.semaphore_wait(barrier, 2 * n - 1 + chips - 1)

    def ring(way, origin, h, k):
        start = snake(origin % n) * fs
        size = fs
        if h == n // 2:
            size = fs // 2
            start = start + way * size
        ref = cap_f.at[core, k, pl.ds(pl.multiple_of(start, fs // 2), size), :]
        return remote(
            ref, ref, ring_send.at[way, h - 1, k], ring_recv.at[way, h - 1, k],
            ((right, left)[way], q),
        )

    def to_sibling(j, k, c):
        rows = pl.ds(pl.multiple_of(snake((pos + j) % n) * fs, fs), fs)
        ref = cap_f.at[c, k, rows, :]
        return remote(ref, ref, sib_send.at[j, k], sib_recv.at[j, k], (i, sibling))

    def send_own(k):
        ring(0, pos, 1, k).start()
        ring(1, pos, 1, k).start()
        to_sibling(0, k, core).start()

    loop(k_n, send_own)

    def forward(k):
        for h in range(1, n // 2):
            ring(0, pos + n - h, h, k).wait_recv()
            ring(0, pos + n - h, h + 1, k).start()
            to_sibling(n - h, k, core).start()
            ring(1, pos + h, h, k).wait_recv()
            ring(1, pos + h, h + 1, k).start()
            to_sibling(h, k, core).start()

    def finish(k):
        for way in range(2):
            ring(way, pos + n // 2, n // 2, k).wait_recv()
        to_sibling(n // 2, k, core).start()

    for a in range(2):
        loads[a].wait()

        def split_rows(b, a=a):
            rows = pl.ds(pl.multiple_of(b * 128, 128), 128)
            hi, lo = split(rows_f[a, rows, :])
            rows_h[a, rows, :] = hi
            rows_l[a, rows, :] = lo

        loop(half // 128, split_rows)
        if a == 0:
            forward(0)

    def stat_copy(offset, source):
        return remote(
            stats.at[source], stats.at[source], st_send.at[offset - 1], st_recv.at[offset - 1],
            group_member(offset),
        )

    def product(a, rb, rhs):
        rows = pl.ds(pl.multiple_of(rb * RB, RB), RB)
        hi = rows_h[a, rows, :]
        lhs = jnp.concatenate([hi, hi, rows_l[a, rows, :]], axis=1)
        return SCALE * jnp.dot(lhs, rhs, preferred_element_type=F32)

    def score_chunk(v):
        k = v // 2
        w = v % 2

        @pl.when(w == 0)
        def _():
            finish(k)

        @pl.when(w == 1)
        def _():
            @pl.when(k + 1 < k_n)
            def _():
                forward(k + 1)

            for j in range(n):
                to_sibling(j, k, 1 - core).wait_recv()

        c = (core + w) % 2
        g = c * k_n + k
        hi, lo = split(cap_f[c, k])
        cap_h[g] = hi
        cap_l[g] = lo
        rhs = jnp.concatenate([cap_h[g], cap_l[g], cap_h[g]], axis=0)

        def bank_block(rb, carry):
            peak, total = carry
            s = product(0, rb, rhs)
            new = jnp.maximum(peak, jnp.max(s, axis=0, keepdims=True))
            total = total * jnp.exp(peak - new) + jnp.sum(jnp.exp(s - new), axis=0, keepdims=True)
            return new, total

        peak, total = lax.fori_loop(
            0, half // RB, bank_block, (jnp.full((1, CW), -1e30, F32), jnp.zeros((1, CW), F32))
        )
        stats[group, 0, pl.ds(g, 1), :] = peak
        stats[group, 1, pl.ds(g, 1), :] = total

        @pl.when(v == 2 * k_n - 1)
        def _():
            for offset in range(1, 2 * n):
                stat_copy(offset, group).start()

        def image_block(rb):
            scores[g, pl.ds(pl.multiple_of(rb * RB, RB), RB), :] = product(1, rb, rhs)

        loop(half // RB, image_block)

    loop(2 * k_n, score_chunk)

    for offset in range(1, 2 * n):
        stat_copy(offset, (group + 2 * n - offset) % (2 * n)).wait_recv()
    peak = stats[0, 0]
    for g in range(1, 2 * n):
        peak = jnp.maximum(peak, stats[g, 0])
    total = jnp.zeros_like(peak)
    for g in range(2 * n):
        total = total + stats[g, 1] * jnp.exp(stats[g, 0] - peak)
    collog[...] = peak + jnp.log(total)

    def weigh(b):
        rows = pl.ds(pl.multiple_of(b * 128, 128), 128)
        best = scores[0, rows, :] - collog[0:1, :]
        for g in range(1, 2 * k_n):
            best = jnp.maximum(best, scores[g, rows, :] - collog[g:g + 1, :])
        m = jnp.max(best, axis=1, keepdims=True)
        total = jnp.zeros((128, CW), F32)
        for g in range(2 * k_n):
            w = jnp.exp(scores[g, rows, :] - collog[g:g + 1, :] - m)
            scores[g, rows, :] = w
            total = total + w
        l = jnp.sum(total, axis=1, keepdims=True)
        ml[z, 0, pl.ds(b, 1), :] = jnp.sum(jnp.where(eye, m, 0.0), axis=0, keepdims=True)
        ml[z, 1, pl.ds(b, 1), :] = jnp.sum(jnp.where(eye, l, 0.0), axis=0, keepdims=True)

    loop(half // 128, weigh)

    def ml_copy(offset, source):
        return remote(
            ml.at[source], ml.at[source], ml_send.at[offset - 1], ml_recv.at[offset - 1],
            chip_member(offset),
        )

    for offset in range(1, chips):
        ml_copy(offset, z).start()

    def average(b):
        starts = [pl.multiple_of(b * 128, 128), pl.multiple_of(side + b * 128, 128)]

        def add(g):
            w = jnp.concatenate([scores[g, pl.ds(s, 128), :] for s in starts], axis=0)
            hi, lo = split(w)
            lhs = jnp.concatenate([hi, hi, lo], axis=1)
            rhs = jnp.concatenate([cap_h[g], cap_l[g], cap_h[g]], axis=1)
            part = lax.dot_general(lhs, rhs, (((1,), (1,)), ((), ())), preferred_element_type=F32)

            @pl.when(g == 0)
            def _():
                for a, s in enumerate(starts):
                    acc[pl.ds(s, 128), :] = part[a * 128:(a + 1) * 128]

            @pl.when(g > 0)
            def _():
                for a, s in enumerate(starts):
                    acc[pl.ds(s, 128), :] += part[a * 128:(a + 1) * 128]

        loop(2 * k_n, add)

        @pl.when(b == 0)
        def _():
            for offset in range(1, chips):
                ml_copy(offset, (z + chips - offset) % chips).wait_recv()
            top = ml[0, 0]
            for c in range(1, chips):
                top = jnp.maximum(top, ml[c, 0])
            whole = jnp.zeros_like(top)
            for c in range(chips):
                whole = whole + ml[c, 1] * jnp.exp(ml[c, 0] - top)
            factor[...] = jnp.exp(ml[z, 0] - top) / whole

        for a, s in enumerate(starts):
            row = factor[pl.ds(a * (side // 128) + b, 1), :]
            column = jnp.sum(jnp.where(eye, row, 0.0), axis=1, keepdims=True)
            acc[pl.ds(s, 128), :] = acc[pl.ds(s, 128), :] * column

    def chunk(way, t):
        return pl.ds(pl.multiple_of(way * side + t * RC, RC), RC)

    def place(way):
        return z if way == 0 else chips - 1 - z

    def step_device(way, by):
        zz = z + by if way == 0 else z - by
        return (i, zz * 2 + core)

    def red_copy(way, t):
        rows = chunk(way, t)
        return remote(
            acc.at[rows, :], red.at[rows, :], red_send.at[way, t], red_recv.at[way, t], step_device(way, 1)
        )

    def bc_copy(way, t, src):
        rows = chunk(way, t)
        return remote(
            src.at[rows, :], fin.at[rows, :], bc_send.at[way, t], bc_recv.at[way, t], step_device(way, -1)
        )

    def out_rows(way, t):
        return pl.ds(pl.multiple_of(core * half + way * side + t * RC, RC), RC)

    def os_copy(way, t, src):
        return remote(
            src.at[chunk(way, t), :], out.at[out_rows(way, t), :],
            os_send.at[way, t], os_recv.at[way, t], (i, sibling),
        )

    def loc_copy(way, t, src):
        return pltpu.make_async_copy(
            src.at[chunk(way, t), :], out.at[out_rows(way, t), :], loc_sem.at[way, t]
        )

    def reduce_step(s):
        for way in range(2):
            zz = place(way)
            t = s - LAG * zz

            @pl.when((t >= 0) & (t < t_n))
            def _(way=way, zz=zz, t=t):
                @pl.when(zz > 0)
                def _():
                    rows = chunk(way, t)
                    red_copy(way, t).wait_recv()
                    acc[rows, :] += red[rows, :]

                @pl.when(zz < chips - 1)
                def _():
                    red_copy(way, t).start()

                @pl.when(zz == chips - 1)
                def _():
                    if chips > 1:
                        bc_copy(way, t, acc).start()
                    os_copy(way, t, acc).start()
                    loc_copy(way, t, acc).start()

            u = s - LAG * (2 * (chips - 1) - zz)

            @pl.when((u >= 0) & (u < t_n) & (zz < chips - 1))
            def _(way=way, zz=zz, u=u):
                bc_copy(way, u, fin).wait_recv()

                @pl.when(zz > 0)
                def _():
                    bc_copy(way, u, fin).start()

                os_copy(way, u, fin).start()
                loc_copy(way, u, fin).start()

    per = 128 // RC

    def block(b):
        average(b)
        loop(per, lambda s: reduce_step(b * per + s))

    loop(t_n // per, block)
    loop(2 * LAG * (chips - 1), lambda s: reduce_step(t_n + s))

    def drain(t):
        for way in range(2):
            zz = place(way)

            @pl.when(zz < chips - 1)
            def _(way=way):
                red_copy(way, t).wait_send()

            @pl.when(zz > 0)
            def _(way=way):
                bc_copy(way, t, fin).wait_send()

            os_copy(way, t, fin).wait_send()
            loc_copy(way, t, fin).wait()
            remote(
                fin.at[chunk(way, t), :],
                out.at[pl.ds(pl.multiple_of((1 - core) * half + way * side + t * RC, RC), RC), :],
                os_send.at[way, t], os_recv.at[way, t], (i, sibling),
            ).wait_recv()

    loop(t_n, drain)

    def drain_gather(k):
        for h in range(1, n // 2 + 1):
            ring(0, pos + n - h + 1, h, k).wait_send()
            ring(1, pos + h - 1, h, k).wait_send()
        for j in range(n):
            to_sibling(j, k, core).wait_send()

    loop(k_n, drain_gather)
    for offset in range(1, 2 * n):
        stat_copy(offset, group).wait_send()
    for offset in range(1, chips):
        ml_copy(offset, z).wait_send()


def local(n, chips, images, captions, bank):
    cap = captions.T
    fs, cl = cap.shape
    d = n * fs
    rows = images.shape[0]
    half = rows // 2
    k_n = cl // CW
    t_n = half // 2 // RC
    dma = pltpu.SemaphoreType.DMA
    any_spec = pl.BlockSpec(memory_space=pl.ANY)
    return pl.pallas_call(
        functools.partial(kernel, n, chips),
        out_shape=jax.ShapeDtypeStruct((rows, d), F32),
        in_specs=[any_spec, any_spec, pl.BlockSpec(memory_space=pltpu.VMEM)],
        out_specs=any_spec,
        scratch_shapes=[
            pltpu.VMEM((2, half, d), F32),
            pltpu.VMEM((2, half, d), BF16),
            pltpu.VMEM((2, half, d), BF16),
            pltpu.VMEM((2, k_n, d, CW), F32),
            pltpu.VMEM((2 * k_n, d, CW), BF16),
            pltpu.VMEM((2 * k_n, d, CW), BF16),
            pltpu.VMEM((2 * k_n, half, CW), F32),
            pltpu.VMEM((half, d), F32),
            pltpu.VMEM((half, d), F32),
            pltpu.VMEM((half, d), F32),
            pltpu.VMEM((2 * n, 2, 2 * k_n, CW), F32),
            pltpu.VMEM((2 * k_n, CW), F32),
            pltpu.VMEM((chips, 2, half // 128, 128), F32),
            pltpu.VMEM((half // 128, 128), F32),
            dma((2,)),
            dma((2, n // 2, k_n)),
            dma((2, n // 2, k_n)),
            dma((n, k_n)),
            dma((n, k_n)),
            dma((2 * n - 1,)),
            dma((2 * n - 1,)),
            dma((chips - 1,)),
            dma((chips - 1,)),
            dma((2, t_n)),
            dma((2, t_n)),
            dma((2, t_n)),
            dma((2, t_n)),
            dma((2, t_n)),
            dma((2, t_n)),
            dma((2, t_n)),
        ],
        compiler_params=pltpu.CompilerParams(
            collective_id=0, has_side_effects=True, vmem_limit_bytes=60 * 1024 * 1024
        ),
        cost_estimate=pl.CostEstimate(
            flops=18 * half * 2 * cl * d, bytes_accessed=12 * rows * d, transcendentals=4 * half * cl
        ),
    )(images, bank, cap)


def solution(mesh):
    return jax.shard_map(
        functools.partial(local, mesh.shape["img"], mesh.shape["cap"] // 2),
        mesh=mesh,
        in_specs=(P("img", None), P("cap", "img"), P("img", None)),
        out_specs=P("img", None),
        check_vma=False,
    )
```

time: 350 us -> 160 us (0.46)
  waiting for transfers between devices: 163 us -> 0 us
  Pallas kernels: 0 us -> 154 us
  matrix products: 110 us -> 0 us
  blocking collectives: 47 us -> 0 us
  other arithmetic: 15.4 us -> 0 us
  between operations: 13.6 us -> 0.01 us
  local copies, waits for them, and re-layouts: 0.01 us -> 5.89 us
    pallas_call x0 -> x1, Pallas kernels: none -> 154 us  [local(): pl.pallas_call(functools.partial(kernel, n, chips), out_shape=jax.ShapeDt...]
    psum x1 -> x0, waiting for transfers between devices: 114 us -> none  [local(): lax.psum((rescaled_affinity(weights, features), jnp.sum(weights, axis=1))...]
    dot_general x3 -> x0, matrix products: 110 us -> none  [the longest x1 59.2 us: rescaled_affinity(): jnp.dot(weights, features, precision=lax.Precision.HIGHEST, preferred_ele...]
    all_gather x1 -> x0, waiting for transfers between devices: 48.6 us -> none  [local(): features = lax.all_gather(captions, 'img', axis=1, tiled=True)]
    psum x2 -> x0, blocking collectives: 23.8 us -> none  [the longest x1 14.9 us: local(): lax.psum((rescaled_affinity(weights, features), jnp.sum(weights, axis=1))...]
    pmax x2 -> x0, blocking collectives: 23.3 us -> none  [the longest x1 13.9 us: local(): top = lax.pmax(row_peak, 'cap')]
    reduce_sum x2 -> x0, other arithmetic: 9.44 us -> none  [the longest x1 5.08 us: local(): jnp.sum(weights, axis=1)]
    div x1 -> x0, other arithmetic: 5.97 us -> none  [local(): result = summed / row_total[:, None]]
  transfers between devices with their start and end apart: 2 -> 0, of which waited for: 2 -> 0; matrix products, arithmetic and copies ran while one was open for 1% -> 0% of each run, Pallas kernels for 0% -> 0%
where the time goes in v1:
time: 160 us
  Pallas kernels  154 us (96%)
  local copies, waits for them, and re-layouts  5.89 us (4%)
    pallas_call x1, Pallas kernels, local(): pl.pallas_call(functools.partial(kernel, n, chips), out_shape=jax.ShapeDt...  154 us
    unnamed x1, local copies, waits for them, and re-layouts  5.89 us

profile of v1, /device:TPU:0, one launch (start us, length us, event | category | flops | bytes accessed | tf_op | source)
XLA Modules:
  0.0 160.2 jit_solution(17516971720571064825)
XLA Ops:
  0.0 154.3 %shard_map.37 = f32[2048,768]{1,0:T(8,128)} custom-call(f32[2048,768]{1,0:T(8,128)} %images.1, f32[2048,768]{1,0:T(8,128)} %bank.1, f32[192,1024]{1,0:T(8,128)} %bitcast.1), custom_call_target="tpu_custom_call" | custom-call | flops 28991029248 | bytes 18874368 | tf_op jit(solution)/shard_map/pallas_call | solution.py:412
  154.3 5.9 %copy.5 = f32[2048,768]{1,0:T(8,128)} copy(f32[2048,768]{1,0:T(8,128)} %shard_map.37) | data formatting | bytes 12582912

commit v2 on v1

--- a/solution.py
+++ b/solution.py
@@ -32,7 +32,7 @@
 def kernel(
     n, chips, images, bank, cap, out,
     rows_f, rows_h, rows_l, cap_f, cap_h, cap_l, scores, acc, red, fin,
-    stats, collog, ml, factor,
+    stats, collog, ml,
     load_sem, ring_send, ring_recv, sib_send, sib_recv, st_send, st_recv, ml_send, ml_recv,
     red_send, red_recv, bc_send, bc_recv, os_send, os_recv, loc_sem,
 ):
@@ -157,6 +157,21 @@
         lhs = jnp.concatenate([hi, hi, rows_l[a, rows, :]], axis=1)
         return SCALE * jnp.dot(lhs, rhs, preferred_element_type=F32)
 
+    def block_starts(b):
+        return [pl.multiple_of(b * 128, 128), pl.multiple_of(side + b * 128, 128)]
+
+    def chunk_rhs(g, axis):
+        hi = cap_h[g]
+        return jnp.concatenate([hi, cap_l[g], hi], axis=axis)
+
+    def image_scores(b, g):
+        parts = []
+        for start in block_starts(b):
+            hi = rows_h[1, pl.ds(start, 128), :]
+            parts.append(jnp.concatenate([hi, hi, rows_l[1, pl.ds(start, 128), :]], axis=1))
+        lhs = jnp.concatenate(parts, axis=0)
+        scores[g] = SCALE * jnp.dot(lhs, chunk_rhs(g, 0), preferred_element_type=F32)
+
     def score_chunk(v):
         k = v // 2
         w = v % 2
@@ -179,7 +194,7 @@
         hi, lo = split(cap_f[c, k])
         cap_h[g] = hi
         cap_l[g] = lo
-        rhs = jnp.concatenate([cap_h[g], cap_l[g], cap_h[g]], axis=0)
+        rhs = chunk_rhs(g, 0)
 
         def bank_block(rb, carry):
             peak, total = carry
@@ -199,10 +214,7 @@
             for offset in range(1, 2 * n):
                 stat_copy(offset, group).start()
 
-        def image_block(rb):
-            scores[g, pl.ds(pl.multiple_of(rb * RB, RB), RB), :] = product(1, rb, rhs)
-
-        loop(half // RB, image_block)
+        image_scores(0, g)
 
     loop(2 * k_n, score_chunk)
 
@@ -217,40 +229,40 @@
     collog[...] = peak + jnp.log(total)
 
     def weigh(b):
-        rows = pl.ds(pl.multiple_of(b * 128, 128), 128)
-        best = scores[0, rows, :] - collog[0:1, :]
-        for g in range(1, 2 * k_n):
-            best = jnp.maximum(best, scores[g, rows, :] - collog[g:g + 1, :])
-        m = jnp.max(best, axis=1, keepdims=True)
-        total = jnp.zeros((128, CW), F32)
-        for g in range(2 * k_n):
-            w = jnp.exp(scores[g, rows, :] - collog[g:g + 1, :] - m)
-            scores[g, rows, :] = w
-            total = total + w
-        l = jnp.sum(total, axis=1, keepdims=True)
-        ml[z, 0, pl.ds(b, 1), :] = jnp.sum(jnp.where(eye, m, 0.0), axis=0, keepdims=True)
-        ml[z, 1, pl.ds(b, 1), :] = jnp.sum(jnp.where(eye, l, 0.0), axis=0, keepdims=True)
-
-    loop(half // 128, weigh)
-
-    def ml_copy(offset, source):
-        return remote(
-            ml.at[source], ml.at[source], ml_send.at[offset - 1], ml_recv.at[offset - 1],
+        def part(a):
+            rows = pl.ds(pl.multiple_of(a * 128, 128), 128)
+            best = scores[0, rows, :] - collog[0:1, :]
+            for g in range(1, 2 * k_n):
+                best = jnp.maximum(best, scores[g, rows, :] - collog[g:g + 1, :])
+            m = jnp.max(best, axis=1, keepdims=True)
+            total = jnp.zeros((128, CW), F32)
+            for g in range(2 * k_n):
+                w = jnp.exp(scores[g, rows, :] - collog[g:g + 1, :] - m)
+                scores[g, rows, :] = w
+                total = total + w
+            l = jnp.sum(total, axis=1, keepdims=True)
+            ml[z, b, pl.ds(a, 1), :] = jnp.sum(jnp.where(eye, m, 0.0), axis=0, keepdims=True)
+            ml[z, b, pl.ds(2 + a, 1), :] = jnp.sum(jnp.where(eye, l, 0.0), axis=0, keepdims=True)
+
+        loop(2, part)
+        for offset in range(1, chips):
+            ml_copy(offset, z, b).start()
+
+    def ml_copy(offset, source, b):
+        return remote(
+            ml.at[source, b], ml.at[source, b], ml_send.at[offset - 1, b], ml_recv.at[offset - 1, b],
             chip_member(offset),
         )
 
-    for offset in range(1, chips):
-        ml_copy(offset, z).start()
-
     def average(b):
-        starts = [pl.multiple_of(b * 128, 128), pl.multiple_of(side + b * 128, 128)]
+        starts = block_starts(b)
 
         def add(g):
-            w = jnp.concatenate([scores[g, pl.ds(s, 128), :] for s in starts], axis=0)
-            hi, lo = split(w)
+            hi, lo = split(scores[g])
             lhs = jnp.concatenate([hi, hi, lo], axis=1)
-            rhs = jnp.concatenate([cap_h[g], cap_l[g], cap_h[g]], axis=1)
-            part = lax.dot_general(lhs, rhs, (((1,), (1,)), ((), ())), preferred_element_type=F32)
+            part = lax.dot_general(
+                lhs, chunk_rhs(g, 1), (((1,), (1,)), ((), ())), preferred_element_type=F32
+            )
 
             @pl.when(g == 0)
             def _():
@@ -264,21 +276,18 @@
 
         loop(2 * k_n, add)
 
-        @pl.when(b == 0)
-        def _():
-            for offset in range(1, chips):
-                ml_copy(offset, (z + chips - offset) % chips).wait_recv()
-            top = ml[0, 0]
-            for c in range(1, chips):
-                top = jnp.maximum(top, ml[c, 0])
-            whole = jnp.zeros_like(top)
-            for c in range(chips):
-                whole = whole + ml[c, 1] * jnp.exp(ml[c, 0] - top)
-            factor[...] = jnp.exp(ml[z, 0] - top) / whole
-
-        for a, s in enumerate(starts):
-            row = factor[pl.ds(a * (side // 128) + b, 1), :]
-            column = jnp.sum(jnp.where(eye, row, 0.0), axis=1, keepdims=True)
+    def normalize(b):
+        for offset in range(1, chips):
+            ml_copy(offset, (z + chips - offset) % chips, b).wait_recv()
+        top = ml[0, b, 0:2, :]
+        for c in range(1, chips):
+            top = jnp.maximum(top, ml[c, b, 0:2, :])
+        whole = jnp.zeros_like(top)
+        for c in range(chips):
+            whole = whole + ml[c, b, 2:4, :] * jnp.exp(ml[c, b, 0:2, :] - top)
+        factor = jnp.exp(ml[z, b, 0:2, :] - top) / whole
+        for a, s in enumerate(block_starts(b)):
+            column = jnp.sum(jnp.where(eye, factor[a:a + 1, :], 0.0), axis=1, keepdims=True)
             acc[pl.ds(s, 128), :] = acc[pl.ds(s, 128), :] * column
 
     def chunk(way, t):
@@ -356,12 +365,31 @@
 
     per = 128 // RC
 
-    def block(b):
-        average(b)
-        loop(per, lambda s: reduce_step(b * per + s))
-
-    loop(t_n // per, block)
-    loop(2 * LAG * (chips - 1), lambda s: reduce_step(t_n + s))
+    def phase(f):
+        b = f // 4
+        part = f % 4
+
+        @pl.when(f < 4 * (side // 128))
+        def _():
+            @pl.when((part == 0) & (b > 0))
+            def _():
+                loop(2 * k_n, lambda g: image_scores(b, g))
+
+            @pl.when(part == 1)
+            def _():
+                weigh(b)
+
+            @pl.when(part == 2)
+            def _():
+                average(b)
+
+            @pl.when(part == 3)
+            def _():
+                normalize(b)
+
+        loop(per // 4, lambda r: reduce_step((f - 3) * (per // 4) + r))
+
+    loop(3 + (t_n + 2 * LAG * (chips - 1)) // (per // 4), phase)
 
     def drain(t):
         for way in range(2):
@@ -396,7 +424,7 @@
     for offset in range(1, 2 * n):
         stat_copy(offset, group).wait_send()
     for offset in range(1, chips):
-        ml_copy(offset, z).wait_send()
+        loop(side // 128, lambda b, offset=offset: ml_copy(offset, z, b).wait_send())
 
 
 def local(n, chips, images, captions, bank):
@@ -421,14 +449,13 @@
             pltpu.VMEM((2, k_n, d, CW), F32),
             pltpu.VMEM((2 * k_n, d, CW), BF16),
             pltpu.VMEM((2 * k_n, d, CW), BF16),
-            pltpu.VMEM((2 * k_n, half, CW), F32),
+            pltpu.VMEM((2 * k_n, 256, CW), F32),
             pltpu.VMEM((half, d), F32),
             pltpu.VMEM((half, d), F32),
             pltpu.VMEM((half, d), F32),
             pltpu.VMEM((2 * n, 2, 2 * k_n, CW), F32),
             pltpu.VMEM((2 * k_n, CW), F32),
-            pltpu.VMEM((chips, 2, half // 128, 128), F32),
-            pltpu.VMEM((half // 128, 128), F32),
+            pltpu.VMEM((chips, half // 256, 4, 128), F32),
             dma((2,)),
             dma((2, n // 2, k_n)),
             dma((2, n // 2, k_n)),
@@ -436,8 +463,8 @@
             dma((n, k_n)),
             dma((2 * n - 1,)),
             dma((2 * n - 1,)),
-            dma((chips - 1,)),
-            dma((chips - 1,)),
+            dma((chips - 1, half // 256)),
+            dma((chips - 1, half // 256)),
             dma((2, t_n)),
             dma((2, t_n)),
             dma((2, t_n)),

time: 160 us -> 158 us (0.988)
  Pallas kernels: 154 us -> 151 us
    pallas_call x1, Pallas kernels: 154 us -> 151 us  [local(): pl.pallas_call(functools.partial(kernel, n, chips), out_shape=jax.ShapeDt...]
where the time goes in v2:
time: 158 us; the launch traced here: 157 us
  Pallas kernels  151 us (96%)
  local copies, waits for them, and re-layouts  5.89 us (4%)
    pallas_call x1, Pallas kernels, local(): pl.pallas_call(functools.partial(kernel, n, chips), out_shape=jax.ShapeDt...  151 us
    unnamed x1, local copies, waits for them, and re-layouts  5.89 us

profile of v2, /device:TPU:0, one launch (start us, length us, event | category | flops | bytes accessed | tf_op | source)
XLA Modules:
  0.0 157.3 jit_solution(5855220572473108769)
XLA Ops:
  0.0 151.4 %shard_map.37 = f32[2048,768]{1,0:T(8,128)} custom-call(f32[2048,768]{1,0:T(8,128)} %images.1, f32[2048,768]{1,0:T(8,128)} %bank.1, f32[192,1024]{1,0:T(8,128)} %bitcast.1), custom_call_target="tpu_custom_call" | custom-call | flops 28991029248 | bytes 18874368 | tf_op jit(solution)/shard_map/pallas_call | solution.py:440
  151.4 5.9 %copy.5 = f32[2048,768]{1,0:T(8,128)} copy(f32[2048,768]{1,0:T(8,128)} %shard_map.37) | data formatting | bytes 12582912

commit v3 on v2

--- a/solution.py
+++ b/solution.py
@@ -10,8 +10,8 @@
 SCALE = 0.03
 CW = 256
 RB = 512
-RC = 32
-LAG = 2
+RC = 16
+LAG = 3
 F32 = jnp.float32
 BF16 = jnp.bfloat16
 
@@ -31,10 +31,10 @@
 
 def kernel(
     n, chips, images, bank, cap, out,
-    rows_f, rows_h, rows_l, cap_f, cap_h, cap_l, scores, acc, red, fin,
+    rows_f, rows_h, rows_l, cap_f, cap_h, cap_l, scores, acc, red,
     stats, collog, ml,
     load_sem, ring_send, ring_recv, sib_send, sib_recv, st_send, st_recv, ml_send, ml_recv,
-    red_send, red_recv, bc_send, bc_recv, os_send, os_recv, loc_sem,
+    red_send, red_recv, bc_send, bc_recv, os_send, os_recv,
 ):
     fs, cl = cap.shape
     d = n * fs
@@ -306,25 +306,16 @@
             acc.at[rows, :], red.at[rows, :], red_send.at[way, t], red_recv.at[way, t], step_device(way, 1)
         )
 
-    def bc_copy(way, t, src):
-        rows = chunk(way, t)
-        return remote(
-            src.at[rows, :], fin.at[rows, :], bc_send.at[way, t], bc_recv.at[way, t], step_device(way, -1)
-        )
-
-    def out_rows(way, t):
-        return pl.ds(pl.multiple_of(core * half + way * side + t * RC, RC), RC)
-
-    def os_copy(way, t, src):
-        return remote(
-            src.at[chunk(way, t), :], out.at[out_rows(way, t), :],
-            os_send.at[way, t], os_recv.at[way, t], (i, sibling),
-        )
-
-    def loc_copy(way, t, src):
-        return pltpu.make_async_copy(
-            src.at[chunk(way, t), :], out.at[out_rows(way, t), :], loc_sem.at[way, t]
-        )
+    def out_rows(way, t, c):
+        return pl.ds(pl.multiple_of(c * half + way * side + t * RC, RC), RC)
+
+    def bc_copy(way, t):
+        ref = out.at[out_rows(way, t, core), :]
+        return remote(ref, ref, bc_send.at[way, t], bc_recv.at[way, t], step_device(way, -1))
+
+    def os_copy(way, t, c):
+        ref = out.at[out_rows(way, t, c), :]
+        return remote(ref, ref, os_send.at[way, t], os_recv.at[way, t], (i, sibling))
 
     def reduce_step(s):
         for way in range(2):
@@ -333,10 +324,14 @@
 
             @pl.when((t >= 0) & (t < t_n))
             def _(way=way, zz=zz, t=t):
+                rows = chunk(way, t)
+
                 @pl.when(zz > 0)
                 def _():
-                    rows = chunk(way, t)
                     red_copy(way, t).wait_recv()
+
+                @pl.when((zz > 0) & (zz < chips - 1))
+                def _():
                     acc[rows, :] += red[rows, :]
 
                 @pl.when(zz < chips - 1)
@@ -345,23 +340,21 @@
 
                 @pl.when(zz == chips - 1)
                 def _():
-                    if chips > 1:
-                        bc_copy(way, t, acc).start()
-                    os_copy(way, t, acc).start()
-                    loc_copy(way, t, acc).start()
+                    out[out_rows(way, t, core), :] = acc[rows, :] + red[rows, :]
+                    bc_copy(way, t).start()
+                    os_copy(way, t, core).start()
 
             u = s - LAG * (2 * (chips - 1) - zz)
 
             @pl.when((u >= 0) & (u < t_n) & (zz < chips - 1))
             def _(way=way, zz=zz, u=u):
-                bc_copy(way, u, fin).wait_recv()
+                bc_copy(way, u).wait_recv()
 
                 @pl.when(zz > 0)
                 def _():
-                    bc_copy(way, u, fin).start()
-
-                os_copy(way, u, fin).start()
-                loc_copy(way, u, fin).start()
+                    bc_copy(way, u).start()
+
+                os_copy(way, u, core).start()
 
     per = 128 // RC
 
@@ -401,15 +394,10 @@
 
             @pl.when(zz > 0)
             def _(way=way):
-                bc_copy(way, t, fin).wait_send()
-
-            os_copy(way, t, fin).wait_send()
-            loc_copy(way, t, fin).wait()
-            remote(
-                fin.at[chunk(way, t), :],
-                out.at[pl.ds(pl.multiple_of((1 - core) * half + way * side + t * RC, RC), RC), :],
-                os_send.at[way, t], os_recv.at[way, t], (i, sibling),
-            ).wait_recv()
+                bc_copy(way, t).wait_send()
+
+            os_copy(way, t, core).wait_send()
+            os_copy(way, t, 1 - core).wait_recv()
 
     loop(t_n, drain)
 
@@ -439,9 +427,9 @@
     any_spec = pl.BlockSpec(memory_space=pl.ANY)
     return pl.pallas_call(
         functools.partial(kernel, n, chips),
-        out_shape=jax.ShapeDtypeStruct((rows, d), F32),
+        out_shape=pltpu.VMEM((rows, d), F32),
         in_specs=[any_spec, any_spec, pl.BlockSpec(memory_space=pltpu.VMEM)],
-        out_specs=any_spec,
+        out_specs=pl.BlockSpec(memory_space=pltpu.VMEM),
         scratch_shapes=[
             pltpu.VMEM((2, half, d), F32),
             pltpu.VMEM((2, half, d), BF16),
@@ -450,7 +438,6 @@
             pltpu.VMEM((2 * k_n, d, CW), BF16),
             pltpu.VMEM((2 * k_n, d, CW), BF16),
             pltpu.VMEM((2 * k_n, 256, CW), F32),
-            pltpu.VMEM((half, d), F32),
             pltpu.VMEM((half, d), F32),
             pltpu.VMEM((half, d), F32),
             pltpu.VMEM((2 * n, 2, 2 * k_n, CW), F32),
@@ -471,10 +458,9 @@
             dma((2, t_n)),
             dma((2, t_n)),
             dma((2, t_n)),
-            dma((2, t_n)),
         ],
         compiler_params=pltpu.CompilerParams(
-            collective_id=0, has_side_effects=True, vmem_limit_bytes=60 * 1024 * 1024
+            collective_id=0, has_side_effects=True, vmem_limit_bytes=48 * 1024 * 1024
         ),
         cost_estimate=pl.CostEstimate(
             flops=18 * half * 2 * cl * d, bytes_accessed=12 * rows * d, transcendentals=4 * half * cl

time: 158 us -> 158 us (level)
  Pallas kernels: 151 us -> 156 us
  local copies, waits for them, and re-layouts: 5.89 us -> 2.71 us
    pallas_call x1, Pallas kernels: 151 us -> 156 us  [local(): pl.pallas_call(functools.partial(kernel, n, chips), out_shape=pltpu.VMEM(...]
    unnamed x1, local copies, waits for them, and re-layouts: 5.89 us -> 2.71 us
where the time goes in v3:
time: 158 us
  Pallas kernels  156 us (99%)
  local copies, waits for them, and re-layouts  2.71 us (2%)
    pallas_call x1, Pallas kernels, local(): pl.pallas_call(functools.partial(kernel, n, chips), out_shape=pltpu.VMEM(...  156 us

profile of v3, /device:TPU:0, one launch (start us, length us, event | category | flops | bytes accessed | tf_op | source)
XLA Modules:
  0.0 158.3 jit_solution(3303060500768857446)
XLA Ops:
  0.0 155.6 %shard_map.37 = f32[2048,768]{1,0:T(8,128)S(1)} custom-call(f32[2048,768]{1,0:T(8,128)} %images.1, f32[2048,768]{1,0:T(8,128)} %bank.1, f32[192,1024]{1,0:T(8,128)} %bitcast.1), custom_call_target="tpu_custom_call" | custom-call | flops 28991029248 | bytes 18874368 | tf_op jit(solution)/shard_map/pallas_call | solution.py:428
  155.6 2.7 %copy.5 = f32[2048,768]{1,0:T(8,128)} copy(f32[2048,768]{1,0:T(8,128)S(1)} %shard_map.37) | data formatting | bytes 12582912

commit v4 on v3

--- a/solution.py
+++ b/solution.py
@@ -10,8 +10,8 @@
 SCALE = 0.03
 CW = 256
 RB = 512
-RC = 16
-LAG = 3
+RC = 32
+LAG = 2
 F32 = jnp.float32
 BF16 = jnp.bfloat16
 
@@ -116,7 +116,7 @@
         ring(1, pos, 1, k).start()
         to_sibling(0, k, core).start()
 
-    loop(k_n, send_own)
+    loop(min(2, k_n), send_own)
 
     def forward(k):
         for h in range(1, n // 2):
@@ -142,8 +142,10 @@
             rows_l[a, rows, :] = lo
 
         loop(half // 128, split_rows)
-        if a == 0:
-            forward(0)
+        if a < k_n:
+            forward(a)
+        if a + 2 < k_n and a == 0:
+            send_own(2)
 
     def stat_copy(offset, source):
         return remote(
@@ -182,9 +184,13 @@
 
         @pl.when(w == 1)
         def _():
-            @pl.when(k + 1 < k_n)
-            def _():
-                forward(k + 1)
+            @pl.when(k + 3 < k_n)
+            def _():
+                send_own(k + 3)
+
+            @pl.when(k + 2 < k_n)
+            def _():
+                forward(k + 2)
 
             for j in range(n):
                 to_sibling(j, k, 1 - core).wait_recv()

time: 158 us -> 146 us (0.924)
  Pallas kernels: 156 us -> 143 us
    pallas_call x1, Pallas kernels: 156 us -> 143 us  [local(): pl.pallas_call(functools.partial(kernel, n, chips), out_shape=pltpu.VMEM(...]
where the time goes in v4:
time: 146 us
  Pallas kernels  143 us (98%)
  local copies, waits for them, and re-layouts  2.71 us (2%)
    pallas_call x1, Pallas kernels, local(): pl.pallas_call(functools.partial(kernel, n, chips), out_shape=pltpu.VMEM(...  143 us

profile of v4, /device:TPU:0, one launch (start us, length us, event | category | flops | bytes accessed | tf_op | source)
XLA Modules:
  0.0 146.0 jit_solution(4645764114520826568)
XLA Ops:
  0.0 143.3 %shard_map.37 = f32[2048,768]{1,0:T(8,128)S(1)} custom-call(f32[2048,768]{1,0:T(8,128)} %images.1, f32[2048,768]{1,0:T(8,128)} %bank.1, f32[192,1024]{1,0:T(8,128)} %bitcast.1), custom_call_target="tpu_custom_call" | custom-call | flops 28991029248 | bytes 18874368 | tf_op jit(solution)/shard_map/pallas_call | solution.py:434
  143.3 2.7 %copy.5 = f32[2048,768]{1,0:T(8,128)} copy(f32[2048,768]{1,0:T(8,128)S(1)} %shard_map.37) | data formatting | bytes 12582912
